TPU v7x, 32 devices: a whole 2x2x4 slice. The times are simulated.
32 devices in a mesh: rep: 8 (over z, x), fsdp: 4 (over y, core).
Axes of the slice: x: 2, y: 2, z: 4, core: 2. Of those that a mesh axis runs over, the one named last changes fastest.
Arguments:
- partial_grads: bfloat16 [32, 512, 8192], P(('rep', 'fsdp')), may hold values from -6 to 6
- momentum: float32 [4096, 8192], P('rep', 'fsdp'), may hold values from -6 to 6
- freq_index: int32 [8, 8, 128, 32], P('rep', None, 'fsdp'), may hold values from 0 to 4095, all different within a row
Outputs:
- new_momentum: float32 [4096, 8192], P('rep', 'fsdp')
- update: float32 [512, 8192], P(None, 'fsdp')
Inputs may be any that keep to these rules, and one draw needn't show every extreme that they name: `freq_index`: the 32 frequencies of one block of one replica are distinct.
All inputs are finite; a program needn't handle non-finite values.
Results may differ from a plain program's by a relative error of at most 0.0003.
Values may be sent and summed in bfloat16 or wider, within the bound.
A program may use at most 128 MiB of HBM per device.

v0:
```python
import jax
import jax.numpy as jnp
from jax import lax
from jax.sharding import PartitionSpec as P

GROUP = 64


momentum_decay = 0.9


def dct_basis(order):
    freq = jnp.arange(order, dtype=jnp.int32)[:, None]
    place = jnp.arange(order, dtype=jnp.int32)[None, :]
    phase = (2 * place + 1) * freq % (4 * order)
    scaling = jnp.where(
        freq == 0, jnp.sqrt(jnp.float32(1.0) / order), jnp.sqrt(jnp.float32(2.0) / order)
    )
    return scaling * jnp.cos(jnp.pi * phase.astype(jnp.float32) / (2.0 * order))


def forward_blocks(field, basis, order):
    row_blocks = field.shape[0] // order
    col_blocks = field.shape[1] // order
    blocks = field.reshape(row_blocks, order, col_blocks, order)
    coef = jnp.einsum("kn,anbm,lm->abkl", basis, blocks, basis, precision=lax.Precision.HIGHEST)
    return coef.reshape(row_blocks, col_blocks, order * order)


def inverse_blocks(coef, basis, order):
    row_blocks, col_blocks = (coef.shape[0], coef.shape[1])
    square = coef.reshape(row_blocks, col_blocks, order, order)
    field = jnp.einsum("kn,abkl,lm->anbm", basis, square, basis, precision=lax.Precision.HIGHEST)
    return field.reshape(row_blocks * order, col_blocks * order)


def select_kept(coef, positions):
    freqs = jnp.arange(coef.shape[2], dtype=jnp.int32)

    def select_one_row(pair):
        row_coef, row_pos = pair
        hits = row_pos[:, :, None] == freqs[None, None, :]
        return jnp.sum(jnp.where(hits, row_coef[:, None, :], jnp.float32(0.0)), axis=2)

    return lax.map(select_one_row, (coef, positions))


def place_values(values, positions, width):
    freqs = jnp.arange(width, dtype=jnp.int32)

    def place_one_row(pair):
        row_vals, row_pos = pair
        hits = row_pos[:, :, None] == freqs[None, None, :]
        return jnp.sum(jnp.where(hits, row_vals[:, :, None], jnp.float32(0.0)), axis=1)

    return lax.map(place_one_row, (values, positions))


def local(partial_grads, momentum, freq_index):
    order = GROUP
    basis = dct_basis(order)
    total_rows = momentum.shape[0]
    blocks_count = 1
    span = total_rows // blocks_count
    span_blocks = span // order
    slab = partial_grads[0, 0:span, :].astype(jnp.float32)
    grad = lax.psum_scatter(slab, "fsdp", scatter_dimension=1, tiled=True)
    field = momentum_decay * momentum + grad
    positions = freq_index[0, 0:span_blocks]
    coef = forward_blocks(field, basis, order)
    width = coef.shape[2]
    kept = select_kept(coef, positions)
    own_dense = place_values(kept, positions, width)
    fresh_parts = field - inverse_blocks(own_dense, basis, order)
    all_values = lax.all_gather(kept[None], "rep", axis=0, tiled=True)
    all_positions = lax.all_gather(positions[None], "rep", axis=0, tiled=True)

    def add_replica(total, pair):
        vals, poss = pair
        return (total + place_values(vals, poss, width), None)

    summed, unused = lax.scan(
        add_replica, jnp.zeros(coef.shape, jnp.float32), (all_values, all_positions)
    )
    update_parts = inverse_blocks(summed, basis, order)
    return (fresh_parts, update_parts)


def solution(mesh):
    return jax.shard_map(
        local,
        mesh=mesh,
        in_specs=(P(("rep", "fsdp"), None, None), P("rep", "fsdp"), P("rep", None, "fsdp", None)),
        out_specs=(P("rep", "fsdp"), P(None, "fsdp")),
        check_vma=False,
    )
```

profile of v0, /device:TPU:0, one launch (start us, length us, event | category | flops | bytes accessed | tf_op | source)
XLA Modules:
  0.0 828.4 jit_solution(3418176128224870292)
XLA Ops:
  7.2 11.3 %bitcast_convert_fusion = f32[512,8192]{1,0:T(8,128)} fusion(bf16[1,512,8192]{2,1,0:T(8,128)(2,1)} %param.11), kind=kLoop, calls=%fused_computation.21 | loop fusion | flops 4194304 | bytes 25165824 | tf_op jit(solution)/shard_map/convert_element_type | solution.py:66
  19.4 34.7 %all_gather.7 = s32[8,8,32,32]{3,2,1,0:T(8,128)S(1)} all-gather(s32[1,8,32,32]{3,2,1,0:T(8,128)S(1)} %copy-done), channel_id=1, replica_groups=mesh['rep'=8,'fsdp'=4] {'rep'}, dimensions={0}, use_global_device_ids=true | all-gather | bytes 294912 | tf_op jit(solution)/shard_map/all_gather | solution.py:76
  54.1 93.5 %reduce-scatter.2.cloned.1.call-done = f32[512,2048]{1,0:T(8,128)} async-done(((f32[512,8192]{1,0:T(8,128)}), f32[512,2048]{1,0:T(8,128)}) %reduce-scatter.2.cloned.1.call-update) | async-done | bytes 4194320 | tf_op jit(solution)/shard_map/reduce_scatter | solution.py:67
  147.5 6.7 multiply_add_fusion
  154.2 8.3 %reshape.53 = f32[8,64,32,64]{3,2,1,0:T(8,128)} reshape(f32[512,2048]{1,0:T(8,128)} %multiply_add_fusion) | data formatting | bytes 8388608 | tf_op jit(solution)/shard_map/reshape | solution.py:25
  162.5 16.2 %fusion.6 = f32[8,32,64,64]{2,3,1,0:T(8,128)S(1)} fusion(f32[8,64,32,64]{3,2,1,0:T(8,128)} %reshape.53, s32[64]{0:T(128)S(1)} %multiply_add_fusion.1, f32[64]{0:T(128)S(1)} %compare_select_fusion), kind=kOutput, calls=%fused_computation.22 | convolution fusion | flops 805367808 | bytes 8389120 | tf_op jit(solution)/shard_map/kn,anbm,lm->abkl/dot_general | solution.py:26
  178.8 9.2 %fusion.23 = f32[8,32,64,64]{3,2,1,0:T(8,128)} fusion(f32[8,32,64,64]{2,3,1,0:T(8,128)S(1)} %fusion.6, s32[64]{0:T(128)S(1)} %multiply_add_fusion.1, f32[64]{0:T(128)S(1)} %compare_select_fusion), kind=kOutput, calls=%fused_computation.41 | convolution fusion | flops 805367808 | bytes 8389120 | tf_op jit(solution)/shard_map/kn,anbm,lm->abkl/dot_general | solution.py:26
  188.0 8.0 reshape.54
  196.0 28.4 %while.50 = (s32[]{:T(128)}, f32[8,32,32]{2,1,0:T(8,128)S(1)}, s32[8,32,32]{2,1,0:T(8,128)S(1)}, f32[8,32,4096]{2,1,0:T(8,128)}) while((s32[]{:T(128)}, f32[8,32,32]{2,1,0:T(8,128)S(1)}, s32[8,32,32]{2,1,0:T(8,128)S(1)}, f32[8,32,4096]{2,1,0:T(8,128)}) %tuple.103), condition=%wide.region_3.4_spmd.clone.clone, body=%wide.region_1.3_spmd.clone.sunk.clone | while | flops 12581890 | bytes 1622081 | solution.py:45
  224.4 32.8 %all-gather = f32[64,32,32]{2,1,0:T(8,128)S(1)} all-gather(f32[8,32,32]{2,1,0:T(8,128)S(1)} %get-tuple-element.366), channel_id=2, replica_groups=mesh['rep'=8,'fsdp'=4] {'rep'}, dimensions={0}, use_global_device_ids=true | all-gather | bytes 294912 | tf_op jit(solution)/shard_map/all_gather | solution.py:75
  257.2 47.0 %while.51 = (s32[]{:T(128)}, f32[8,32,4096]{2,1,0:T(8,128)}, s32[8,32,32]{2,1,0:T(8,128)S(1)}, f32[8,32,32]{2,1,0:T(8,128)S(1)}) while((s32[]{:T(128)}, f32[8,32,4096]{2,1,0:T(8,128)}, s32[8,32,32]{2,1,0:T(8,128)S(1)}, f32[8,32,32]{2,1,0:T(8,128)S(1)}) %tuple.104), condition=%wide.region_6.7_spmd.clone.clone, body=%wide.region_4.6_spmd.clone.sunk.clone | while | flops 12451842 | bytes 1598013 | solution.py:56
  304.2 7.9 reshape.55
  312.0 10.7 %fusion.21 = f32[8,32,64,64]{2,3,1,0:T(8,128)S(1)} fusion(f32[8,32,64,64]{3,2,1,0:T(8,128)} %reshape.55, s32[64]{0:T(128)S(1)} %multiply_add_fusion.1, f32[64]{0:T(128)S(1)} %compare_select_fusion), kind=kOutput, calls=%fused_computation.40 | convolution fusion | flops 805367808 | bytes 8389120 | tf_op jit(solution)/shard_map/kn,abkl,lm->anbm/dot_general | solution.py:33
  322.7 8.4 %convolution_bitcast_fusion.1 = f32[8,64,32,64]{3,1,2,0:T(8,128)S(1)} fusion(f32[8,32,64,64]{2,3,1,0:T(8,128)S(1)} %fusion.21, s32[64]{0:T(128)S(1)} %multiply_add_fusion.1, f32[64]{0:T(128)S(1)} %compare_select_fusion), kind=kOutput, calls=%fused_computation.26 | convolution fusion | flops 805367808 | bytes 8389120 | tf_op jit(solution)/shard_map/kn,abkl,lm->anbm/dot_general | solution.py:33
  331.1 8.0 copy.19
  339.1 7.8 reshape.56
  346.9 6.6 sub.3
  353.5 425.2 %while.53 = (s32[]{:T(128)}, f32[8,32,4096]{2,1,0:T(8,128)}, f32[8,8,32,32]{3,2,1,0:T(8,128)S(1)}, s32[8,8,32,32]{3,2,1,0:T(8,128)S(1)}, s32[]{:T(128)}, /*index=5*/s32[]{:T(128)}, f32[]{:T(128)}) while((s32[]{:T(128)}, f32[8,32,4096]{2,1,0:T(8,128)}, f32[8,8,32,32]{3,2,1,0:T(8,128)S(1)}, ...), condition=%wide.region_11.12_spmd.clone.clone, body=%wide.region_7.11_spmd.clone.sunk.clone | while | flops 14548997 | bytes 14312148 | solution.py:82
  353.9 47.0 %while.52 = (s32[]{:T(128)}, f32[8,32,4096]{2,1,0:T(8,128)}, s32[8,32,32]{2,1,0:T(8,128)S(1)}, f32[8,32,32]{2,1,0:T(8,128)S(1)}, s32[]{:T(128)}) while((s32[]{:T(128)}, f32[8,32,4096]{2,1,0:T(8,128)}, s32[8,32,32]{2,1,0:T(8,128)S(1)}, f32[8,32,32]{2,1,0:T(8,128)S(1)}, s32[]{:T(128)}) %tuple.88), condition=%wide.region_10.10_spmd.clone, body=%wide.region_8.9_spmd.clone.sunk | while | flops 12451842 | bytes 1598021 | solution.py:56
  405.9 47.0 %while.52 = (s32[]{:T(128)}, f32[8,32,4096]{2,1,0:T(8,128)}, s32[8,32,32]{2,1,0:T(8,128)S(1)}, f32[8,32,32]{2,1,0:T(8,128)S(1)}, s32[]{:T(128)}) while((s32[]{:T(128)}, f32[8,32,4096]{2,1,0:T(8,128)}, s32[8,32,32]{2,1,0:T(8,128)S(1)}, f32[8,32,32]{2,1,0:T(8,128)S(1)}, s32[]{:T(128)}) %tuple.88), condition=%wide.region_10.10_spmd.clone, body=%wide.region_8.9_spmd.clone.sunk | while | flops 12451842 | bytes 1598021 | solution.py:56
  459.2 47.0 %while.52 = (s32[]{:T(128)}, f32[8,32,4096]{2,1,0:T(8,128)}, s32[8,32,32]{2,1,0:T(8,128)S(1)}, f32[8,32,32]{2,1,0:T(8,128)S(1)}, s32[]{:T(128)}) while((s32[]{:T(128)}, f32[8,32,4096]{2,1,0:T(8,128)}, s32[8,32,32]{2,1,0:T(8,128)S(1)}, f32[8,32,32]{2,1,0:T(8,128)S(1)}, s32[]{:T(128)}) %tuple.88), condition=%wide.region_10.10_spmd.clone, body=%wide.region_8.9_spmd.clone.sunk | while | flops 12451842 | bytes 1598021 | solution.py:56
  512.4 47.0 %while.52 = (s32[]{:T(128)}, f32[8,32,4096]{2,1,0:T(8,128)}, s32[8,32,32]{2,1,0:T(8,128)S(1)}, f32[8,32,32]{2,1,0:T(8,128)S(1)}, s32[]{:T(128)}) while((s32[]{:T(128)}, f32[8,32,4096]{2,1,0:T(8,128)}, s32[8,32,32]{2,1,0:T(8,128)S(1)}, f32[8,32,32]{2,1,0:T(8,128)S(1)}, s32[]{:T(128)}) %tuple.88), condition=%wide.region_10.10_spmd.clone, body=%wide.region_8.9_spmd.clone.sunk | while | flops 12451842 | bytes 1598021 | solution.py:56
  559.5 6.2 select_add_fusion.3
  565.7 47.0 %while.52 = (s32[]{:T(128)}, f32[8,32,4096]{2,1,0:T(8,128)}, s32[8,32,32]{2,1,0:T(8,128)S(1)}, f32[8,32,32]{2,1,0:T(8,128)S(1)}, s32[]{:T(128)}) while((s32[]{:T(128)}, f32[8,32,4096]{2,1,0:T(8,128)}, s32[8,32,32]{2,1,0:T(8,128)S(1)}, f32[8,32,32]{2,1,0:T(8,128)S(1)}, s32[]{:T(128)}) %tuple.88), condition=%wide.region_10.10_spmd.clone, body=%wide.region_8.9_spmd.clone.sunk | while | flops 12451842 | bytes 1598021 | solution.py:56
  618.9 47.0 %while.52 = (s32[]{:T(128)}, f32[8,32,4096]{2,1,0:T(8,128)}, s32[8,32,32]{2,1,0:T(8,128)S(1)}, f32[8,32,32]{2,1,0:T(8,128)S(1)}, s32[]{:T(128)}) while((s32[]{:T(128)}, f32[8,32,4096]{2,1,0:T(8,128)}, s32[8,32,32]{2,1,0:T(8,128)S(1)}, f32[8,32,32]{2,1,0:T(8,128)S(1)}, s32[]{:T(128)}) %tuple.88), condition=%wide.region_10.10_spmd.clone, body=%wide.region_8.9_spmd.clone.sunk | while | flops 12451842 | bytes 1598021 | solution.py:56
  672.2 47.0 %while.52 = (s32[]{:T(128)}, f32[8,32,4096]{2,1,0:T(8,128)}, s32[8,32,32]{2,1,0:T(8,128)S(1)}, f32[8,32,32]{2,1,0:T(8,128)S(1)}, s32[]{:T(128)}) while((s32[]{:T(128)}, f32[8,32,4096]{2,1,0:T(8,128)}, s32[8,32,32]{2,1,0:T(8,128)S(1)}, f32[8,32,32]{2,1,0:T(8,128)S(1)}, s32[]{:T(128)}) %tuple.88), condition=%wide.region_10.10_spmd.clone, body=%wide.region_8.9_spmd.clone.sunk | while | flops 12451842 | bytes 1598021 | solution.py:56
  725.5 47.0 %while.52 = (s32[]{:T(128)}, f32[8,32,4096]{2,1,0:T(8,128)}, s32[8,32,32]{2,1,0:T(8,128)S(1)}, f32[8,32,32]{2,1,0:T(8,128)S(1)}, s32[]{:T(128)}) while((s32[]{:T(128)}, f32[8,32,4096]{2,1,0:T(8,128)}, s32[8,32,32]{2,1,0:T(8,128)S(1)}, f32[8,32,32]{2,1,0:T(8,128)S(1)}, s32[]{:T(128)}) %tuple.88), condition=%wide.region_10.10_spmd.clone, body=%wide.region_8.9_spmd.clone.sunk | while | flops 12451842 | bytes 1598021 | solution.py:56
  778.7 7.9 reshape.57
  786.5 10.7 %fusion.18 = f32[8,32,64,64]{2,3,1,0:T(8,128)S(1)} fusion(f32[8,32,64,64]{3,2,1,0:T(8,128)} %reshape.57, s32[64]{0:T(128)S(1)} %multiply_add_fusion.1, f32[64]{0:T(128)S(1)} %compare_select_fusion), kind=kOutput, calls=%fused_computation.39 | convolution fusion | flops 805367808 | bytes 8389120 | tf_op jit(solution)/shard_map/kn,abkl,lm->anbm/dot_general | solution.py:33
  797.2 8.3 %convolution_bitcast_fusion = f32[8,64,32,64]{3,1,2,0:T(8,128)S(1)} fusion(f32[8,32,64,64]{2,3,1,0:T(8,128)S(1)} %fusion.18, s32[64]{0:T(128)S(1)} %multiply_add_fusion.1, f32[64]{0:T(128)S(1)} %compare_select_fusion), kind=kOutput, calls=%fused_computation.25 | convolution fusion | flops 805367808 | bytes 8389120 | tf_op jit(solution)/shard_map/kn,abkl,lm->anbm/dot_general | solution.py:33
  805.6 8.0 copy.22
  813.6 7.8 reshape.58
  (360 shorter events, 493.7 us)
Async XLA Ops:
  7.2 140.4 %reduce-scatter.2.cloned.1.call-start = ((), (), s32[]{:S(2)}) async-start(), calls=%async_computation.1 | async-start | bytes 20971520 | tf_op jit(solution)/shard_map/reduce_scatter | solution.py:67
  18.5 0.9 copy-start
Sparse Core Ops, SparseCore 0:
  18.7 128.8 reduce-scatter.1
where the time goes:
time: 832 us; the launch traced here: 828 us
  other arithmetic  454 us (55%)
  local copies, waits for them, and re-layouts  134 us (16%)
  waiting for transfers between devices  93.5 us (11%)
  blocking collectives  67.5 us (8%)
  matrix products  63.5 us (8%)
  between operations  14.3 us (2%)
    reduce_sum x72, other arithmetic, place_one_row(): jnp.sum(jnp.where(hits, row_vals[:, :, None], jnp.float32(0.0)), axis=1)  362 us
    reduce_scatter x1, waiting for transfers between devices, local(): grad = lax.psum_scatter(slab, 'fsdp', scatter_dimension=1, tiled=True)  93.5 us
    dynamic_update_slice x72, local copies, waits for them, and re-layouts, place_values(): return lax.map(place_one_row, (values, positions))  60 us
    add x8, other arithmetic, add_replica(): return (total + place_values(vals, poss, width), None)  48.1 us
    dot_general x4, matrix products, inverse_blocks(): jnp.einsum('kn,abkl,lm->anbm', basis, square, basis, precision=lax.Precis...  38.1 us
    all_gather x1, blocking collectives, local(): all_positions = lax.all_gather(positions[None], 'rep', axis=0, tiled=True)  34.7 us
    all_gather x1, blocking collectives, local(): all_values = lax.all_gather(kept[None], 'rep', axis=0, tiled=True)  32.8 us
    dot_general x2, matrix products, forward_blocks(): jnp.einsum('kn,anbm,lm->abkl', basis, blocks, basis, precision=lax.Precis...  25.4 us
  transfers between devices with their start and end apart: 1, of which 1 were waited for; matrix products, arithmetic and copies ran while one was open for 0% of the time, Pallas kernels for 0%

commit v1 on v0

v1 whole, which is shorter than its diff:
```python
import functools

import jax
import jax.numpy as jnp
import ml_dtypes
import numpy as np
from jax import lax
from jax.experimental import pallas as pl
from jax.experimental.pallas import tpu as pltpu
from jax.sharding import PartitionSpec as P

ORDER = 64
PACK = 4
WIDE = PACK * ORDER
MOMENTUM_DECAY = 0.9
MESH = pl.DeviceIdType.MESH
F32 = jnp.float32
BF16 = jnp.bfloat16
LEVELS = 32767.0


def constants():
    k = np.arange(ORDER)[:, None]
    n = np.arange(ORDER)[None, :]
    scale = np.where(k == 0, np.sqrt(1.0 / ORDER), np.sqrt(2.0 / ORDER))
    basis = (scale * np.cos(np.pi * ((2 * n + 1) * k % (4 * ORDER)) / (2.0 * ORDER))).astype(np.float32)

    def halves(matrix):
        high = matrix.astype(ml_dtypes.bfloat16)
        low = (matrix - high.astype(np.float32)).astype(ml_dtypes.bfloat16)
        return high, low

    def left(matrix):
        high, low = halves(matrix)
        return np.concatenate([high, low, high, np.zeros_like(high)], axis=1)

    eye = np.eye(PACK, dtype=np.float32)
    stack = [*halves(np.kron(eye, basis.T)), *halves(np.kron(eye, basis)), left(basis), left(basis.T)]
    return np.concatenate([m.astype(np.float32) for m in stack], axis=0)


def halves(x):
    high = x.astype(BF16)
    low = (x - high.astype(F32)).astype(BF16)
    return high, low


def mm(a, b):
    return lax.dot_general(a, b, (((1,), (0,)), ((), ())), preferred_element_type=F32)


def mm_nt(a, b):
    return lax.dot_general(a, b, (((1,), (1,)), ((), ())), preferred_element_type=F32)


def right_times(x, w_high, w_low):
    high, low = halves(x)
    both = mm(jnp.concatenate([high, low], axis=0), w_high)
    return both[:ORDER] + both[ORDER:] + mm(high, w_low)


def left_times(w, x):
    high, low = halves(x)
    return mm(w, jnp.concatenate([high, high, low], axis=0))


def hot_columns(pos, keep):
    lanes = pos.shape[1]
    lane = lax.broadcasted_iota(jnp.int32, (1, lanes), 1)
    block = lax.rem(lane, keep * PACK) // keep
    spot = block * ORDER + jnp.bitwise_and(pos, ORDER - 1)
    rows = lax.broadcasted_iota(jnp.int32, (WIDE, lanes), 0)
    return jnp.where(rows == spot, 1.0, 0.0).astype(BF16)


def hot_rows(pos):
    rows = lax.broadcasted_iota(jnp.int32, (ORDER, pos.shape[1]), 0)
    return rows == jnp.right_shift(pos, 6)


def kernel(
    nr, nq, na, ng, width, keep,
    pg, mom, idx, table, nm_out, up_out,
    wide_table, rf_high, rf_low, ri_high, ri_low, left_fwd, left_inv, table_sem,
    gbuf, pbuf, sbuf, rbuf, sscale, rscale, mbuf, ubuf, gidx, gval,
    own_sem, mom_sem, nm_sem, up_sem, pair_send, pair_recv,
    y_send, y_recv, ys_send, ys_recv, idx_send, idx_recv, val_send, val_recv,
):
    rep = lax.axis_index("rep")
    me = lax.axis_index("fsdp")
    chip = me // 2
    core = lax.rem(me, 2)
    partner = 2 * chip + 1 - core

    def rep_at(d):
        return lax.rem(rep + d, nr)

    def chip_at(d):
        return lax.rem(chip + d, nq)

    def rows(a):
        return pl.ds(pl.multiple_of(a * ORDER, ORDER), ORDER)

    def part(d, a, c):
        col = pl.multiple_of((2 * chip_at(d) + c) * width, width)
        return pg.at[0, rows(a), pl.ds(col, width)]

    def own_copy(d, a):
        return pltpu.make_async_copy(part(d, a, core), gbuf.at[d, a], own_sem.at[d, a])

    def mom_copy(a):
        return pltpu.make_async_copy(mom.at[rows(a), :], mbuf.at[a], mom_sem.at[a])

    def nm_copy(a):
        return pltpu.make_async_copy(mbuf.at[a], nm_out.at[rows(a), :], nm_sem.at[a])

    def up_copy(a):
        return pltpu.make_async_copy(ubuf.at[a], up_out.at[rows(a), :], up_sem.at[a])

    def pair_copy(d, a):
        return pltpu.make_async_remote_copy(
            part(d, a, 1 - core), pbuf.at[d, a], pair_send.at[d, a], pair_recv.at[d, a],
            device_id=(rep, partner), device_id_type=MESH)

    def y_copy(d, a):
        return pltpu.make_async_remote_copy(
            sbuf.at[d - 1, a], rbuf.at[d - 1, a], y_send.at[d - 1, a], y_recv.at[d - 1, a],
            device_id=(rep, 2 * chip_at(d) + core), device_id_type=MESH)

    def ys_copy(d, a):
        return pltpu.make_async_remote_copy(
            sscale.at[d - 1, a], rscale.at[d - 1, a], ys_send.at[d - 1, a], ys_recv.at[d - 1, a],
            device_id=(rep, 2 * chip_at(d) + core), device_id_type=MESH)

    def idx_copy(d):
        return pltpu.make_async_remote_copy(
            idx, gidx.at[d], idx_send.at[d], idx_recv.at[d],
            device_id=(rep_at(d), me), device_id_type=MESH)

    def val_copy(d, a):
        return pltpu.make_async_remote_copy(
            gval.at[0, a], gval.at[d, a], val_send.at[d, a], val_recv.at[d, a],
            device_id=(rep_at(d), me), device_id_type=MESH)

    def each(count, body):
        def step(i, carry):
            body(i)
            return carry
        lax.fori_loop(0, count, step, 0)

    table_copy = pltpu.make_async_copy(table, wide_table, table_sem)
    table_copy.start()

    def start_local(a):
        for d in range(1, nq):
            own_copy(d, a).start()
    each(na, start_local)

    barrier = pltpu.get_barrier_semaphore()
    pl.semaphore_signal(barrier, inc=1, device_id=(rep, partner), device_id_type=MESH)
    for d in range(1, nq):
        pl.semaphore_signal(barrier, inc=1, device_id=(rep, 2 * chip_at(d) + core), device_id_type=MESH)
    for d in range(1, nr):
        pl.semaphore_signal(barrier, inc=1, device_id=(rep_at(d), me), device_id_type=MESH)
    pl.semaphore_wait(barrier, nq + nr - 1)

    def start_pairs(a):
        for d in range(1, nq):
            pair_copy(d, a).start()
    each(na, start_pairs)

    def start_rest(a):
        pair_copy(0, a).start()
        own_copy(0, a).start()
        mom_copy(a).start()
    each(na, start_rest)

    def send_sums(a):
        for d in range(1, nq):
            own_copy(d, a).wait()
            pair_copy(d, a).wait_recv()

            def encode(g):
                cols = pl.ds(pl.multiple_of(g * WIDE, WIDE), WIDE)
                total = gbuf[d, a, :, cols].astype(F32) + pbuf[d, a, :, cols].astype(F32)
                top = jnp.maximum(jnp.max(jnp.abs(total), axis=0, keepdims=True), 1e-30)
                sscale[d - 1, a, :, cols] = top * (1.0 / LEVELS)
                sbuf[d - 1, a, :, cols] = jnp.round(total * (LEVELS / top)).astype(jnp.int32).astype(jnp.int16)
            each(ng, encode)
            y_copy(d, a).start()
            ys_copy(d, a).start()
    each(na, send_sums)

    for d in range(1, nr):
        idx_copy(d).start()
    gidx[0] = idx[...]

    table_copy.wait()
    for i, target in enumerate((rf_high, rf_low, ri_high, ri_low)):
        target[...] = wide_table[i * WIDE:(i + 1) * WIDE, :].astype(BF16)
    for i, target in enumerate((left_fwd, left_inv)):
        start = 4 * WIDE + i * ORDER
        target[...] = wide_table[start:start + ORDER, 0:3 * ORDER].astype(BF16)

    def find_kept(a):
        own_copy(0, a).wait()
        pair_copy(0, a).wait_recv()
        mom_copy(a).wait()
        for d in range(1, nq):
            y_copy(d, a).wait_recv()
            ys_copy(d, a).wait_recv()

        def one(g):
            cols = pl.ds(pl.multiple_of(g * WIDE, WIDE), WIDE)
            field = gbuf[0, a, :, cols].astype(F32) + pbuf[0, a, :, cols].astype(F32)
            for d in range(1, nq):
                field += rbuf[d - 1, a, :, cols].astype(jnp.int32).astype(F32) * rscale[d - 1, a, :, cols]
            field += MOMENTUM_DECAY * mbuf[a, :, cols]
            mbuf[a, :, cols] = field
            coef = left_times(left_fwd[...], right_times(field, rf_high[...], rf_low[...]))
            pos = gidx[0, a, pl.ds(g, 1), :]
            high, low = halves(coef)
            picked = mm(jnp.concatenate([high, low], axis=0), hot_columns(pos, keep))
            picked = picked[:ORDER] + picked[ORDER:]
            kept = jnp.sum(jnp.where(hot_rows(pos), picked, 0.0), axis=0, keepdims=True)
            gval[0, a, pl.ds(g, 1), :] = kept
        each(ng, one)
        for d in range(1, nr):
            val_copy(d, a).start()

    def decode(pos, val):
        high, low = halves(val)
        hot = hot_rows(pos)
        placed = jnp.concatenate(
            [jnp.where(hot, high.astype(F32), 0.0).astype(BF16), jnp.where(hot, low.astype(F32), 0.0).astype(BF16)], axis=0)
        dense = mm_nt(placed, hot_columns(pos, keep))
        dense = dense[:ORDER] + dense[ORDER:]
        return left_times(left_inv[...], right_times(dense, ri_high[...], ri_low[...]))

    def remove_kept(a):
        def one(g):
            cols = pl.ds(pl.multiple_of(g * WIDE, WIDE), WIDE)
            row = pl.ds(g, 1)
            mbuf[a, :, cols] = mbuf[a, :, cols] - decode(gidx[0, a, row, :], gval[0, a, row, :])
        each(ng, one)
        nm_copy(a).start()

    def add_up(a):
        for d in range(1, nr):
            val_copy(d, a).wait_recv()

        def one(g):
            cols = pl.ds(pl.multiple_of(g * WIDE, WIDE), WIDE)
            row = pl.ds(g, 1)
            pos = jnp.concatenate([gidx[d, a, row, :] for d in range(nr)], axis=1)
            val = jnp.concatenate([gval[d, a, row, :] for d in range(nr)], axis=1)
            ubuf[a, :, cols] = decode(pos, val)
        each(ng, one)
        up_copy(a).start()

    find_kept(0)
    remove_kept(0)
    for d in range(1, nr):
        idx_copy(d).wait_recv()

    def step(i):
        find_kept(i + 1)
        remove_kept(i + 1)
        add_up(i)
    each(na - 1, step)
    add_up(na - 1)

    def drain(a):
        for d in range(nq):
            pair_copy(d, a).wait_send()
        for d in range(1, nq):
            y_copy(d, a).wait_send()
            ys_copy(d, a).wait_send()
        for d in range(1, nr):
            val_copy(d, a).wait_send()
        nm_copy(a).wait()
        up_copy(a).wait()
    each(na, drain)
    for d in range(1, nr):
        idx_copy(d).wait_send()


def local(nr, nf, partial_grads, momentum, freq_index):
    total_rows, width = momentum.shape
    na = total_rows // ORDER
    ng = width // WIDE
    nq = nf // 2
    keep = freq_index.shape[3]
    lanes = PACK * keep
    idx = freq_index.reshape(na, ng, lanes)
    table = jnp.asarray(constants())
    dma = pltpu.SemaphoreType.DMA
    vmem = pl.BlockSpec(memory_space=pltpu.VMEM)
    hbm = pl.BlockSpec(memory_space=pl.ANY)
    return pl.pallas_call(
        functools.partial(kernel, nr, nq, na, ng, width, keep),
        out_shape=(
            jax.ShapeDtypeStruct((total_rows, width), F32),
            jax.ShapeDtypeStruct((total_rows, width), F32),
        ),
        in_specs=[hbm, hbm, vmem, hbm],
        out_specs=(hbm, hbm),
        scratch_shapes=[
            pltpu.VMEM(table.shape, F32),
            pltpu.VMEM((WIDE, WIDE), BF16), pltpu.VMEM((WIDE, WIDE), BF16),
            pltpu.VMEM((WIDE, WIDE), BF16), pltpu.VMEM((WIDE, WIDE), BF16),
            pltpu.VMEM((ORDER, 3 * ORDER), BF16), pltpu.VMEM((ORDER, 3 * ORDER), BF16),
            dma,
            pltpu.VMEM((nq, na, ORDER, width), BF16),
            pltpu.VMEM((nq, na, ORDER, width), BF16),
            pltpu.VMEM((nq - 1, na, ORDER, width), jnp.int16),
            pltpu.VMEM((nq - 1, na, ORDER, width), jnp.int16),
            pltpu.VMEM((nq - 1, na, 1, width), F32),
            pltpu.VMEM((nq - 1, na, 1, width), F32),
            pltpu.VMEM((na, ORDER, width), F32),
            pltpu.VMEM((na, ORDER, width), F32),
            pltpu.VMEM((nr, na, ng, lanes), jnp.int32),
            pltpu.VMEM((nr, na, ng, lanes), F32),
            dma((nq, na)), dma((na,)), dma((na,)), dma((na,)),
            dma((nq, na)), dma((nq, na)),
            dma((nq - 1, na)), dma((nq - 1, na)), dma((nq - 1, na)), dma((nq - 1, na)),
            dma((nr,)), dma((nr,)), dma((nr, na)), dma((nr, na)),
        ],
        compiler_params=pltpu.CompilerParams(
            collective_id=0, has_side_effects=True, vmem_limit_bytes=50 * 1024 * 1024),
        cost_estimate=pl.CostEstimate(
            flops=20 * 10**9, bytes_accessed=28 * 2**20, transcendentals=0),
    )(partial_grads, momentum, idx, table)


def solution(mesh):
    return jax.shard_map(
        functools.partial(local, mesh.shape["rep"], mesh.shape["fsdp"]),
        mesh=mesh,
        in_specs=(P(("rep", "fsdp"), None, None), P("rep", "fsdp"), P("rep", None, "fsdp", None)),
        out_specs=(P("rep", "fsdp"), P(None, "fsdp")),
        check_vma=False,
    )
```

time: 832 us -> 135 us (0.16)
  other arithmetic: 454 us -> 0 us
  Pallas kernels: 0 us -> 125 us
  local copies, waits for them, and re-layouts: 134 us -> 9.12 us
  waiting for transfers between devices: 93.5 us -> 0 us
  blocking collectives: 67.5 us -> 0 us
  matrix products: 63.5 us -> 0 us
  between operations: 14.3 us -> 0.66 us
    reduce_sum x80 -> x0, other arithmetic: 381 us -> none  [the longest x72 362 us: place_one_row(): jnp.sum(jnp.where(hits, row_vals[:, :, None], jnp.float32(0.0)), axis=1)]
    pallas_call x0 -> x1, Pallas kernels: none -> 125 us  [local(): pl.pallas_call(functools.partial(kernel, nr, nq, na, ng, width, keep), ou...]
    reduce_scatter x1 -> x0, waiting for transfers between devices: 93.5 us -> none  [local(): grad = lax.psum_scatter(slab, 'fsdp', scatter_dimension=1, tiled=True)]
    all_gather x2 -> x0, blocking collectives: 67.5 us -> none  [the longest x1 34.7 us: local(): all_positions = lax.all_gather(positions[None], 'rep', axis=0, tiled=True)]
    dot_general x6 -> x0, matrix products: 63.5 us -> none  [the longest x4 38.1 us: inverse_blocks(): jnp.einsum('kn,abkl,lm->anbm', basis, square, basis, precision=lax.Precis...]
    dynamic_update_slice x80 -> x0, local copies, waits for them, and re-layouts: 60.1 us -> none  [the longest x72 60 us: place_values(): return lax.map(place_one_row, (values, positions))]
    add x10 -> x0, other arithmetic: 54.8 us -> none  [the longest x8 48.1 us: add_replica(): return (total + place_values(vals, poss, width), None)]
    reshape x6 -> x1, local copies, waits for them, and re-layouts: 47.7 us -> 0.99 us  [local(): idx = freq_index.reshape(na, ng, lanes)]
  transfers between devices with their start and end apart: 1 -> 0, of which waited for: 1 -> 0; matrix products, arithmetic and copies ran while one was open for 0% -> 0% of each run, Pallas kernels for 0% -> 0%
where the time goes in v1:
time: 135 us
  Pallas kernels  125 us (93%)
  local copies, waits for them, and re-layouts  9.12 us (7%)
    pallas_call x1, Pallas kernels, local(): pl.pallas_call(functools.partial(kernel, nr, nq, na, ng, width, keep), ou...  125 us
    unnamed x6, local copies, waits for them, and re-layouts  8.13 us

profile of v1, /device:TPU:0, one launch (start us, length us, event | category | flops | bytes accessed | tf_op | source)
XLA Modules:
  0.0 134.7 jit_solution(11061577272711008195)
XLA Ops:
  0.6 1.0 reshape.7.idx
  1.6 0.0 copy-start
  1.6 1.3 copy-done
  2.9 124.9 %shard_map.59 = (f32[512,2048]{1,0:T(8,128)}, f32[512,2048]{1,0:T(8,128)}) custom-call(bf16[1,512,8192]{2,1,0:T(8,128)(2,1)} %pg.1, f32[512,2048]{1,0:T(8,128)} %mom.1, s32[8,8,128]{2,1,0:T(8,128)S(1)} %reshape.7.idx, f32[1152,256]{1,0:T(8,128)S(1)} %copy-done), custom_call_target="tpu_custom_call" | custom-call | flops 20000000000 | bytes 29360128 | tf_op jit(solution)/shard_map/pallas_call | solution.py:300
  127.9 0.0 copy-start.1
  127.9 4.8 %copy.8 = f32[512,2048]{1,0:T(8,128)} copy(f32[512,2048]{1,0:T(8,128)} %get-tuple-element.4) | data formatting | bytes 8388608
  132.7 0.0 copy-done.1
  132.7 2.0 %copy.9 = f32[512,2048]{1,0:T(8,128)} copy(f32[512,2048]{1,0:T(8,128)S(1)} %copy-done.1) | data formatting | bytes 8388608
Async XLA Ops:
  1.6 1.3 copy-start
  127.9 4.9 %copy-start.1 = (f32[512,2048]{1,0:T(8,128)S(1)}, f32[512,2048]{1,0:T(8,128)}, u32[]{:S(2)}) copy-start(f32[512,2048]{1,0:T(8,128)} %get-tuple-element.5) | copy-start | bytes 12582916

commit v2 on v1

v2 whole, which is shorter than its diff:
```python
import functools

import jax
import jax.numpy as jnp
import numpy as np
from jax import lax
from jax.experimental import pallas as pl
from jax.experimental.pallas import tpu as pltpu
from jax.sharding import PartitionSpec as P

ORDER = 64
PACK = 4
WIDE = PACK * ORDER
MOMENTUM_DECAY = 0.9
MESH = pl.DeviceIdType.MESH
F32 = jnp.float32
BF16 = jnp.bfloat16
LEVELS = 32767.0


def constants():
    k = np.arange(ORDER)[:, None]
    n = np.arange(ORDER)[None, :]
    scale = np.where(k == 0, np.sqrt(1.0 / ORDER), np.sqrt(2.0 / ORDER))
    basis = (scale * np.cos(np.pi * ((2 * n + 1) * k % (4 * ORDER)) / (2.0 * ORDER))).astype(np.float32)

    return np.tile(np.concatenate([basis.T, basis], axis=0), (1, PACK))


def halves(x):
    high = x.astype(BF16)
    low = (x - high.astype(F32)).astype(BF16)
    return high, low


def mm(a, b):
    return lax.dot_general(a, b, (((1,), (0,)), ((), ())), preferred_element_type=F32)


def mm_nt(a, b):
    return lax.dot_general(a, b, (((1,), (1,)), ((), ())), preferred_element_type=F32)


def right_times(x, w_high, w_low):
    high, low = halves(x)
    both = mm(jnp.concatenate([high, low], axis=0), w_high)
    return both[:ORDER] + both[ORDER:] + mm(high, w_low)


def left_times(w, x):
    high, low = halves(x)
    return mm(w, jnp.concatenate([high, high, low], axis=0))


def hot_columns(pos, keep):
    lanes = pos.shape[1]
    lane = lax.broadcasted_iota(jnp.int32, (1, lanes), 1)
    block = lax.rem(lane, keep * PACK) // keep
    spot = block * ORDER + jnp.bitwise_and(pos, ORDER - 1)
    rows = lax.broadcasted_iota(jnp.int32, (WIDE, lanes), 0)
    return jnp.where(rows == spot, 1.0, 0.0).astype(BF16)


def hot_rows(pos):
    rows = lax.broadcasted_iota(jnp.int32, (ORDER, pos.shape[1]), 0)
    return rows == jnp.right_shift(pos, 6)


def kernel(
    nr, nq, na, ng, width, keep,
    pg, mom, idx, table, mbuf, ubuf,
    rf_high, rf_low, ri_high, ri_low, left_fwd, left_inv,
    gbuf, pbuf, sbuf, rbuf, sscale, rscale, gidx, gval,
    own_sem, mom_sem, pair_send, pair_recv,
    y_send, y_recv, ys_send, ys_recv, idx_send, idx_recv, val_send, val_recv,
):
    rep = lax.axis_index("rep")
    me = lax.axis_index("fsdp")
    chip = me // 2
    core = lax.rem(me, 2)
    partner = 2 * chip + 1 - core

    def rep_at(d):
        return lax.rem(rep + d, nr)

    def chip_at(d):
        return lax.rem(chip + d, nq)

    def rows(a):
        return pl.ds(pl.multiple_of(a * ORDER, ORDER), ORDER)

    def part(d, a, c):
        col = pl.multiple_of((2 * chip_at(d) + c) * width, width)
        return pg.at[0, rows(a), pl.ds(col, width)]

    def own_copy(d, a):
        return pltpu.make_async_copy(part(d, a, core), gbuf.at[d, a], own_sem.at[d, a])

    def mom_copy(a):
        return pltpu.make_async_copy(mom.at[rows(a), :], mbuf.at[rows(a), :], mom_sem.at[a])

    def pair_copy(d, a):
        return pltpu.make_async_remote_copy(
            part(d, a, 1 - core), pbuf.at[d, a], pair_send.at[d, a], pair_recv.at[d, a],
            device_id=(rep, partner), device_id_type=MESH)

    def y_copy(d, a):
        return pltpu.make_async_remote_copy(
            sbuf.at[d - 1, a], rbuf.at[d - 1, a], y_send.at[d - 1, a], y_recv.at[d - 1, a],
            device_id=(rep, 2 * chip_at(d) + core), device_id_type=MESH)

    def ys_copy(d, a):
        return pltpu.make_async_remote_copy(
            sscale.at[d - 1, a], rscale.at[d - 1, a], ys_send.at[d - 1, a], ys_recv.at[d - 1, a],
            device_id=(rep, 2 * chip_at(d) + core), device_id_type=MESH)

    def idx_copy(d):
        return pltpu.make_async_remote_copy(
            idx, gidx.at[d], idx_send.at[d], idx_recv.at[d],
            device_id=(rep_at(d), me), device_id_type=MESH)

    def val_copy(d, a):
        return pltpu.make_async_remote_copy(
            gval.at[0, a], gval.at[d, a], val_send.at[d, a], val_recv.at[d, a],
            device_id=(rep_at(d), me), device_id_type=MESH)

    def each(count, body):
        def step(i, carry):
            body(i)
            return carry
        lax.fori_loop(0, count, step, 0)

    def start_local(a):
        for d in range(1, nq):
            own_copy(d, a).start()
    each(na, start_local)

    barrier = pltpu.get_barrier_semaphore()
    pl.semaphore_signal(barrier, inc=1, device_id=(rep, partner), device_id_type=MESH)
    for d in range(1, nq):
        pl.semaphore_signal(barrier, inc=1, device_id=(rep, 2 * chip_at(d) + core), device_id_type=MESH)
    for d in range(1, nr):
        pl.semaphore_signal(barrier, inc=1, device_id=(rep_at(d), me), device_id_type=MESH)
    pl.semaphore_wait(barrier, nq + nr - 1)

    def start_pairs(a):
        for d in range(1, nq):
            pair_copy(d, a).start()
    each(na, start_pairs)

    def start_rest(a):
        pair_copy(0, a).start()
        own_copy(0, a).start()
        mom_copy(a).start()
    each(na, start_rest)

    span = (2 if ng % 2 == 0 else 1) * WIDE

    def send_sums(a):
        for d in range(1, nq):
            own_copy(d, a).wait()
            pair_copy(d, a).wait_recv()

            def encode(g):
                cols = pl.ds(pl.multiple_of(g * span, span), span)
                total = gbuf[d, a, :, cols].astype(F32) + pbuf[d, a, :, cols].astype(F32)
                top = jnp.maximum(jnp.max(jnp.abs(total), axis=0, keepdims=True), 1e-30)
                sscale[d - 1, a, :, cols] = top * (1.0 / LEVELS)
                sbuf[d - 1, a, :, cols] = jnp.round(total * (LEVELS / top)).astype(jnp.int32).astype(jnp.int16)
            each(width // span, encode)
            y_copy(d, a).start()
            ys_copy(d, a).start()
    each(na, send_sums)

    for d in range(1, nr):
        idx_copy(d).start()
    gidx[0] = idx[...]

    def blocks_of(shape):
        row = lax.broadcasted_iota(jnp.int32, shape, 0) // ORDER
        return row, lax.broadcasted_iota(jnp.int32, shape, 1) // ORDER

    row_block, col_block = blocks_of((WIDE, WIDE))
    for i, (high, low) in enumerate(((rf_high, rf_low), (ri_high, ri_low))):
        tiled = table[i * ORDER:(i + 1) * ORDER, :]
        wide = jnp.where(row_block == col_block, jnp.concatenate([tiled] * PACK, axis=0), 0.0)
        high[...], low[...] = halves(wide)
    _, col_block = blocks_of((ORDER, WIDE))
    for i, target in enumerate((left_inv, left_fwd)):
        tiled = table[i * ORDER:(i + 1) * ORDER, :]
        high = tiled.astype(BF16).astype(F32)
        target[...] = jnp.where(col_block == 1, tiled - high, high).astype(BF16)[:, :3 * ORDER]

    for d in range(1, nr):
        idx_copy(d).wait_recv()

    ways = 4 if ng % 4 == 0 else (2 if ng % 2 == 0 else 1)

    def groups(body):
        def some(i):
            gs = [i * ways + w for w in range(ways)]
            body(gs, [pl.ds(pl.multiple_of(g * WIDE, WIDE), WIDE) for g in gs], [pl.ds(g, 1) for g in gs])
        each(ng // ways, some)

    def right_all(xs, w_high, w_low):
        split = [halves(x) for x in xs]
        high = jnp.concatenate([h for h, _ in split], axis=0)
        low = jnp.concatenate([l for _, l in split], axis=0)
        out = mm(high, w_high) + (mm(low, w_high) + mm(high, w_low))
        return [out[w * ORDER:(w + 1) * ORDER] for w in range(len(xs))]

    def find_kept(a):
        own_copy(0, a).wait()
        pair_copy(0, a).wait_recv()
        mom_copy(a).wait()
        for d in range(1, nq):
            y_copy(d, a).wait_recv()
            ys_copy(d, a).wait_recv()

        def some(gs, cols, row):
            field = [gbuf[0, a, :, c].astype(F32) + pbuf[0, a, :, c].astype(F32) for c in cols]
            for d in range(1, nq):
                field = [f + rbuf[d - 1, a, :, c].astype(jnp.int32).astype(F32) * rscale[d - 1, a, :, c]
                         for f, c in zip(field, cols)]
            field = [f + MOMENTUM_DECAY * mbuf[rows(a), c] for f, c in zip(field, cols)]
            pos = [gidx[0, a, r, :] for r in row]
            for f, c in zip(field, cols):
                mbuf[rows(a), c] = f
            half = right_all(field, rf_high[...], rf_low[...])
            coef = [halves(left_times(left_fwd[...], h)) for h in half]
            picked = [mm(jnp.concatenate(c, axis=0), hot_columns(p, keep)) for c, p in zip(coef, pos)]
            kept = [jnp.sum(jnp.where(hot_rows(p), x[:ORDER] + x[ORDER:], 0.0), axis=0, keepdims=True)
                    for x, p in zip(picked, pos)]
            for r, k in zip(row, kept):
                gval[0, a, r, :] = k
        groups(some)
        for d in range(1, nr):
            val_copy(d, a).start()

    def decode(pos, val):
        dense = []
        for p, v in zip(pos, val):
            high, low = halves(v)
            hot = hot_rows(p)
            placed = jnp.concatenate(
                [jnp.where(hot, x.astype(F32), 0.0).astype(BF16) for x in (high, low)], axis=0)
            both = mm_nt(placed, hot_columns(p, keep))
            dense.append(both[:ORDER] + both[ORDER:])
        half = right_all(dense, ri_high[...], ri_low[...])
        return [left_times(left_inv[...], h) for h in half]

    def remove_kept(a):
        def some(gs, cols, row):
            field = [mbuf[rows(a), c] for c in cols]
            part = decode([gidx[0, a, r, :] for r in row], [gval[0, a, r, :] for r in row])
            for f, x, c in zip(field, part, cols):
                mbuf[rows(a), c] = f - x
        groups(some)

    def add_up(a):
        for d in range(1, nr):
            val_copy(d, a).wait_recv()

        def some(gs, cols, row):
            pos = [jnp.concatenate([gidx[d, a, r, :] for d in range(nr)], axis=1) for r in row]
            val = [jnp.concatenate([gval[d, a, r, :] for d in range(nr)], axis=1) for r in row]
            for x, c in zip(decode(pos, val), cols):
                ubuf[rows(a), c] = x
        groups(some)

    def step(i):
        @pl.when(i < na)
        def _():
            find_kept(i)
            remove_kept(i)

        @pl.when(i > 0)
        def _():
            add_up(i - 1)
    each(na + 1, step)

    def drain(a):
        for d in range(nq):
            pair_copy(d, a).wait_send()
        for d in range(1, nq):
            y_copy(d, a).wait_send()
            ys_copy(d, a).wait_send()
        for d in range(1, nr):
            val_copy(d, a).wait_send()
    each(na, drain)
    for d in range(1, nr):
        idx_copy(d).wait_send()


def local(nr, nf, partial_grads, momentum, freq_index):
    total_rows, width = momentum.shape
    na = total_rows // ORDER
    ng = width // WIDE
    nq = nf // 2
    keep = freq_index.shape[3]
    lanes = PACK * keep
    idx = freq_index.reshape(na, ng, lanes)
    table = jnp.asarray(constants())
    dma = pltpu.SemaphoreType.DMA
    vmem = pl.BlockSpec(memory_space=pltpu.VMEM)
    hbm = pl.BlockSpec(memory_space=pltpu.HBM)
    return pl.pallas_call(
        functools.partial(kernel, nr, nq, na, ng, width, keep),
        out_shape=(
            jax.ShapeDtypeStruct((total_rows, width), F32),
            jax.ShapeDtypeStruct((total_rows, width), F32),
        ),
        in_specs=[hbm, hbm, vmem, vmem],
        out_specs=(vmem, vmem),
        scratch_shapes=[
            pltpu.VMEM((WIDE, WIDE), BF16), pltpu.VMEM((WIDE, WIDE), BF16),
            pltpu.VMEM((WIDE, WIDE), BF16), pltpu.VMEM((WIDE, WIDE), BF16),
            pltpu.VMEM((ORDER, 3 * ORDER), BF16), pltpu.VMEM((ORDER, 3 * ORDER), BF16),
            pltpu.VMEM((nq, na, ORDER, width), BF16),
            pltpu.VMEM((nq, na, ORDER, width), BF16),
            pltpu.VMEM((nq - 1, na, ORDER, width), jnp.int16),
            pltpu.VMEM((nq - 1, na, ORDER, width), jnp.int16),
            pltpu.VMEM((nq - 1, na, 1, width), F32),
            pltpu.VMEM((nq - 1, na, 1, width), F32),
            pltpu.VMEM((nr, na, ng, lanes), jnp.int32),
            pltpu.VMEM((nr, na, ng, lanes), F32),
            dma((nq, na)), dma((na,)),
            dma((nq, na)), dma((nq, na)),
            dma((nq - 1, na)), dma((nq - 1, na)), dma((nq - 1, na)), dma((nq - 1, na)),
            dma((nr,)), dma((nr,)), dma((nr, na)), dma((nr, na)),
        ],
        compiler_params=pltpu.CompilerParams(
            collective_id=0, has_side_effects=True, vmem_limit_bytes=43 * 1024 * 1024),
        cost_estimate=pl.CostEstimate(
            flops=20 * 10**9, bytes_accessed=28 * 2**20, transcendentals=0),
    )(partial_grads, momentum, idx, table)


def solution(mesh):
    return jax.shard_map(
        functools.partial(local, mesh.shape["rep"], mesh.shape["fsdp"]),
        mesh=mesh,
        in_specs=(P(("rep", "fsdp"), None, None), P("rep", "fsdp"), P("rep", None, "fsdp", None)),
        out_specs=(P("rep", "fsdp"), P(None, "fsdp")),
        check_vma=False,
    )
```

time: 135 us -> 73.3 us (0.54)
  Pallas kernels: 125 us -> 66.5 us
  local copies, waits for them, and re-layouts: 9.12 us -> 5.92 us
    pallas_call x1, Pallas kernels: 125 us -> 66.5 us  [local(): pl.pallas_call(functools.partial(kernel, nr, nq, na, ng, width, keep), ou...]
    unnamed x6 -> x4, local copies, waits for them, and re-layouts: 8.13 us -> 4.93 us
where the time goes in v2:
time: 73.3 us; the launch traced here: 73.1 us
  Pallas kernels  66.5 us (91%)
  local copies, waits for them, and re-layouts  5.92 us (8%)
    pallas_call x1, Pallas kernels, local(): pl.pallas_call(functools.partial(kernel, nr, nq, na, ng, width, keep), ou...  66.5 us
    unnamed x4, local copies, waits for them, and re-layouts  4.93 us

profile of v2, /device:TPU:0, one launch (start us, length us, event | category | flops | bytes accessed | tf_op | source)
XLA Modules:
  0.0 73.1 jit_solution(9769180817143696529)
XLA Ops:
  0.6 1.0 %reshape.7.idx = s32[8,8,128]{2,1,0:T(8,128)S(1)} reshape(s32[1,8,32,32]{3,2,1,0:T(8,128)} %param.6) | data formatting | bytes 65536 | tf_op jit(solution)/shard_map/reshape | solution.py:302
  1.6 0.0 copy-start
  1.6 0.9 %copy-done = f32[128,256]{1,0:T(8,128)S(1)} copy-done((f32[128,256]{1,0:T(8,128)S(1)}, f32[128,256]{1,0:T(8,128)}, u32[]{:S(2)}) %copy-start) | copy-done | bytes 131096
  2.5 66.5 %shard_map.59 = (f32[512,2048]{1,0:T(8,128)S(1)}, f32[512,2048]{1,0:T(8,128)S(1)}) custom-call(bf16[1,512,8192]{2,1,0:T(8,128)(2,1)} %pg.1, f32[512,2048]{1,0:T(8,128)} %mom.1, s32[8,8,128]{2,1,0:T(8,128)S(1)} %reshape.7.idx, f32[128,256]{1,0:T(8,128)S(1)} %copy-done), custom_call_target="tpu_custom_call" | custom-call | flops 20000000000 | bytes 29360128 | tf_op jit(solution)/shard_map/pallas_call | solution.py:307
  69.1 2.0 %copy.8 = f32[512,2048]{1,0:T(8,128)} copy(f32[512,2048]{1,0:T(8,128)S(1)} %get-tuple-element.4) | data formatting | bytes 8388608
  71.1 2.0 %copy.9 = f32[512,2048]{1,0:T(8,128)} copy(f32[512,2048]{1,0:T(8,128)S(1)} %get-tuple-element.5) | data formatting | bytes 8388608
Async XLA Ops:
  1.6 0.9 %copy-start = (f32[128,256]{1,0:T(8,128)S(1)}, f32[128,256]{1,0:T(8,128)}, u32[]{:S(2)}) copy-start(f32[128,256]{1,0:T(8,128)} %constant.2.clone.table) | copy-start | bytes 393220

commit v3 on v2

--- a/solution.py
+++ b/solution.py
@@ -1,8 +1,8 @@
 import functools
+import math
 
 import jax
 import jax.numpy as jnp
-import numpy as np
 from jax import lax
 from jax.experimental import pallas as pl
 from jax.experimental.pallas import tpu as pltpu
@@ -18,13 +18,17 @@
 LEVELS = 32767.0
 
 
-def constants():
-    k = np.arange(ORDER)[:, None]
-    n = np.arange(ORDER)[None, :]
-    scale = np.where(k == 0, np.sqrt(1.0 / ORDER), np.sqrt(2.0 / ORDER))
-    basis = (scale * np.cos(np.pi * ((2 * n + 1) * k % (4 * ORDER)) / (2.0 * ORDER))).astype(np.float32)
-
-    return np.tile(np.concatenate([basis.T, basis], axis=0), (1, PACK))
+def tiled_basis(transposed):
+    row = lax.broadcasted_iota(jnp.int32, (ORDER, WIDE), 0)
+    lane = jnp.bitwise_and(lax.broadcasted_iota(jnp.int32, (ORDER, WIDE), 1), ORDER - 1)
+    freq, place = (lane, row) if transposed else (row, lane)
+    turn = jnp.bitwise_and((2 * place + 1) * freq, 4 * ORDER - 1)
+    x = (jnp.abs(turn - 2 * ORDER) - ORDER).astype(F32) * (math.pi / (2 * ORDER))
+    square = x * x
+    series = jnp.ones_like(x)
+    for power in (14, 12, 10, 8, 6, 4, 2):
+        series = 1.0 - square * series * (1.0 / (power * (power + 1)))
+    return jnp.where(freq == 0, math.sqrt(1.0 / ORDER), math.sqrt(2.0 / ORDER)) * (x * series)
 
 
 def halves(x):
@@ -68,7 +72,7 @@
 
 def kernel(
     nr, nq, na, ng, width, keep,
-    pg, mom, idx, table, mbuf, ubuf,
+    pg, mom, idx, mbuf, ubuf,
     rf_high, rf_low, ri_high, ri_low, left_fwd, left_inv,
     gbuf, pbuf, sbuf, rbuf, sscale, rscale, gidx, gval,
     own_sem, mom_sem, pair_send, pair_recv,
@@ -182,19 +186,19 @@
 
     row_block, col_block = blocks_of((WIDE, WIDE))
     for i, (high, low) in enumerate(((rf_high, rf_low), (ri_high, ri_low))):
-        tiled = table[i * ORDER:(i + 1) * ORDER, :]
+        tiled = tiled_basis(i == 0)
         wide = jnp.where(row_block == col_block, jnp.concatenate([tiled] * PACK, axis=0), 0.0)
         high[...], low[...] = halves(wide)
     _, col_block = blocks_of((ORDER, WIDE))
     for i, target in enumerate((left_inv, left_fwd)):
-        tiled = table[i * ORDER:(i + 1) * ORDER, :]
+        tiled = tiled_basis(i == 0)
         high = tiled.astype(BF16).astype(F32)
         target[...] = jnp.where(col_block == 1, tiled - high, high).astype(BF16)[:, :3 * ORDER]
 
     for d in range(1, nr):
         idx_copy(d).wait_recv()
 
-    ways = 4 if ng % 4 == 0 else (2 if ng % 2 == 0 else 1)
+    ways = max(w for w in (1, 2, 4, 8) if ng % w == 0)
 
     def groups(body):
         def some(i):
@@ -269,14 +273,14 @@
         groups(some)
 
     def step(i):
+        @pl.when(i > 0)
+        def _():
+            add_up(i - 1)
+
         @pl.when(i < na)
         def _():
             find_kept(i)
             remove_kept(i)
-
-        @pl.when(i > 0)
-        def _():
-            add_up(i - 1)
     each(na + 1, step)
 
     def drain(a):
@@ -300,7 +304,6 @@
     keep = freq_index.shape[3]
     lanes = PACK * keep
     idx = freq_index.reshape(na, ng, lanes)
-    table = jnp.asarray(constants())
     dma = pltpu.SemaphoreType.DMA
     vmem = pl.BlockSpec(memory_space=pltpu.VMEM)
     hbm = pl.BlockSpec(memory_space=pltpu.HBM)
@@ -310,7 +313,7 @@
             jax.ShapeDtypeStruct((total_rows, width), F32),
             jax.ShapeDtypeStruct((total_rows, width), F32),
         ),
-        in_specs=[hbm, hbm, vmem, vmem],
+        in_specs=[hbm, hbm, vmem],
         out_specs=(vmem, vmem),
         scratch_shapes=[
             pltpu.VMEM((WIDE, WIDE), BF16), pltpu.VMEM((WIDE, WIDE), BF16),
@@ -333,7 +336,7 @@
             collective_id=0, has_side_effects=True, vmem_limit_bytes=43 * 1024 * 1024),
         cost_estimate=pl.CostEstimate(
             flops=20 * 10**9, bytes_accessed=28 * 2**20, transcendentals=0),
-    )(partial_grads, momentum, idx, table)
+    )(partial_grads, momentum, idx)
 
 
 def solution(mesh):

time: 73.3 us -> 83.3 us (1.14)
  Pallas kernels: 66.5 us -> 77.5 us
  local copies, waits for them, and re-layouts: 5.92 us -> 5.02 us
    pallas_call x1, Pallas kernels: 66.5 us -> 77.5 us  [local(): pl.pallas_call(functools.partial(kernel, nr, nq, na, ng, width, keep), ou...]
    unnamed x4 -> x2, local copies, waits for them, and re-layouts: 4.93 us -> 4.03 us
where the time goes in v3:
time: 83.3 us; the launch traced here: 83.2 us
  Pallas kernels  77.5 us (93%)
  local copies, waits for them, and re-layouts  5.02 us (6%)
    pallas_call x1, Pallas kernels, local(): pl.pallas_call(functools.partial(kernel, nr, nq, na, ng, width, keep), ou...  77.5 us
    unnamed x2, local copies, waits for them, and re-layouts  4.03 us

profile of v3, /device:TPU:0, one launch (start us, length us, event | category | flops | bytes accessed | tf_op | source)
XLA Modules:
  0.0 83.2 jit_solution(3302940340854196439)
XLA Ops:
  0.6 1.0 %reshape.7.idx = s32[8,8,128]{2,1,0:T(8,128)S(1)} reshape(s32[1,8,32,32]{3,2,1,0:T(8,128)} %param.5) | data formatting | bytes 65536 | tf_op jit(solution)/shard_map/reshape | solution.py:306
  1.6 77.5 %shard_map.50 = (f32[512,2048]{1,0:T(8,128)S(1)}, f32[512,2048]{1,0:T(8,128)S(1)}) custom-call(bf16[1,512,8192]{2,1,0:T(8,128)(2,1)} %pg.1, f32[512,2048]{1,0:T(8,128)} %mom.1, s32[8,8,128]{2,1,0:T(8,128)S(1)} %reshape.7.idx), custom_call_target="tpu_custom_call" | custom-call | flops 20000000000 | bytes 29360128 | tf_op jit(solution)/shard_map/pallas_call | solution.py:310
  79.2 2.0 %copy.7 = f32[512,2048]{1,0:T(8,128)} copy(f32[512,2048]{1,0:T(8,128)S(1)} %get-tuple-element.4) | data formatting | bytes 8388608
  81.2 2.0 %copy.8 = f32[512,2048]{1,0:T(8,128)} copy(f32[512,2048]{1,0:T(8,128)S(1)} %get-tuple-element.5) | data formatting | bytes 8388608

commit v4 on v3

--- a/solution.py
+++ b/solution.py
@@ -198,7 +198,7 @@
     for d in range(1, nr):
         idx_copy(d).wait_recv()
 
-    ways = max(w for w in (1, 2, 4, 8) if ng % w == 0)
+    ways = max(w for w in (1, 2, 4) if ng % w == 0)
 
     def groups(body):
         def some(i):
@@ -212,6 +212,18 @@
         low = jnp.concatenate([l for _, l in split], axis=0)
         out = mm(high, w_high) + (mm(low, w_high) + mm(high, w_low))
         return [out[w * ORDER:(w + 1) * ORDER] for w in range(len(xs))]
+
+    def decode(pos, val, hots):
+        dense = []
+        for p, v, columns in zip(pos, val, hots):
+            high, low = halves(v)
+            hot = hot_rows(p)
+            placed = jnp.concatenate(
+                [jnp.where(hot, x.astype(F32), 0.0).astype(BF16) for x in (high, low)], axis=0)
+            both = mm_nt(placed, columns)
+            dense.append(both[:ORDER] + both[ORDER:])
+        half = right_all(dense, ri_high[...], ri_low[...])
+        return [left_times(left_inv[...], h) for h in half]
 
     def find_kept(a):
         own_copy(0, a).wait()
@@ -228,39 +240,20 @@
                          for f, c in zip(field, cols)]
             field = [f + MOMENTUM_DECAY * mbuf[rows(a), c] for f, c in zip(field, cols)]
             pos = [gidx[0, a, r, :] for r in row]
-            for f, c in zip(field, cols):
-                mbuf[rows(a), c] = f
+            hots = [hot_columns(p, keep) for p in pos]
             half = right_all(field, rf_high[...], rf_low[...])
             coef = [halves(left_times(left_fwd[...], h)) for h in half]
-            picked = [mm(jnp.concatenate(c, axis=0), hot_columns(p, keep)) for c, p in zip(coef, pos)]
+            picked = [mm(jnp.concatenate(c, axis=0), h) for c, h in zip(coef, hots)]
             kept = [jnp.sum(jnp.where(hot_rows(p), x[:ORDER] + x[ORDER:], 0.0), axis=0, keepdims=True)
                     for x, p in zip(picked, pos)]
             for r, k in zip(row, kept):
                 gval[0, a, r, :] = k
+            for f, x, c in zip(field, decode(pos, kept, hots), cols):
+                mbuf[rows(a), c] = f - x
         groups(some)
         for d in range(1, nr):
             val_copy(d, a).start()
 
-    def decode(pos, val):
-        dense = []
-        for p, v in zip(pos, val):
-            high, low = halves(v)
-            hot = hot_rows(p)
-            placed = jnp.concatenate(
-                [jnp.where(hot, x.astype(F32), 0.0).astype(BF16) for x in (high, low)], axis=0)
-            both = mm_nt(placed, hot_columns(p, keep))
-            dense.append(both[:ORDER] + both[ORDER:])
-        half = right_all(dense, ri_high[...], ri_low[...])
-        return [left_times(left_inv[...], h) for h in half]
-
-    def remove_kept(a):
-        def some(gs, cols, row):
-            field = [mbuf[rows(a), c] for c in cols]
-            part = decode([gidx[0, a, r, :] for r in row], [gval[0, a, r, :] for r in row])
-            for f, x, c in zip(field, part, cols):
-                mbuf[rows(a), c] = f - x
-        groups(some)
-
     def add_up(a):
         for d in range(1, nr):
             val_copy(d, a).wait_recv()
@@ -268,19 +261,19 @@
         def some(gs, cols, row):
             pos = [jnp.concatenate([gidx[d, a, r, :] for d in range(nr)], axis=1) for r in row]
             val = [jnp.concatenate([gval[d, a, r, :] for d in range(nr)], axis=1) for r in row]
-            for x, c in zip(decode(pos, val), cols):
+            hots = [hot_columns(p, keep) for p in pos]
+            for x, c in zip(decode(pos, val, hots), cols):
                 ubuf[rows(a), c] = x
         groups(some)
 
     def step(i):
+        @pl.when(i < na)
+        def _():
+            find_kept(i)
+
         @pl.when(i > 0)
         def _():
             add_up(i - 1)
-
-        @pl.when(i < na)
-        def _():
-            find_kept(i)
-            remove_kept(i)
     each(na + 1, step)
 
     def drain(a):

time: 83.3 us -> 72.3 us (0.87)
  Pallas kernels: 77.5 us -> 66.5 us
    pallas_call x1, Pallas kernels: 77.5 us -> 66.5 us  [local(): pl.pallas_call(functools.partial(kernel, nr, nq, na, ng, width, keep), ou...]
where the time goes in v4:
time: 72.3 us; the launch traced here: 72.1 us
  Pallas kernels  66.5 us (92%)
  local copies, waits for them, and re-layouts  5.02 us (7%)
    pallas_call x1, Pallas kernels, local(): pl.pallas_call(functools.partial(kernel, nr, nq, na, ng, width, keep), ou...  66.5 us
    unnamed x2, local copies, waits for them, and re-layouts  4.03 us

profile of v4, /device:TPU:0, one launch (start us, length us, event | category | flops | bytes accessed | tf_op | source)
XLA Modules:
  0.0 72.1 jit_solution(6624412966233530890)
XLA Ops:
  0.6 1.0 %reshape.7.idx = s32[8,8,128]{2,1,0:T(8,128)S(1)} reshape(s32[1,8,32,32]{3,2,1,0:T(8,128)} %param.5) | data formatting | bytes 65536 | tf_op jit(solution)/shard_map/reshape | solution.py:299
  1.6 66.5 %shard_map.50 = (f32[512,2048]{1,0:T(8,128)S(1)}, f32[512,2048]{1,0:T(8,128)S(1)}) custom-call(bf16[1,512,8192]{2,1,0:T(8,128)(2,1)} %pg.1, f32[512,2048]{1,0:T(8,128)} %mom.1, s32[8,8,128]{2,1,0:T(8,128)S(1)} %reshape.7.idx), custom_call_target="tpu_custom_call" | custom-call | flops 20000000000 | bytes 29360128 | tf_op jit(solution)/shard_map/pallas_call | solution.py:303
  68.1 2.0 %copy.7 = f32[512,2048]{1,0:T(8,128)} copy(f32[512,2048]{1,0:T(8,128)S(1)} %get-tuple-element.4) | data formatting | bytes 8388608
  70.1 2.0 %copy.8 = f32[512,2048]{1,0:T(8,128)} copy(f32[512,2048]{1,0:T(8,128)S(1)} %get-tuple-element.5) | data formatting | bytes 8388608
